TPU v7x, 512 devices: a whole 4x8x8 slice. The times are simulated.
512 devices in a mesh: row: 32 (over y, x), col: 16 (over z, core).
Axes of the slice: x: 4, y: 8, z: 8, core: 2. Of those that a mesh axis runs over, the one named last changes fastest.
Arguments:
- source_features: bfloat16 [16, 2048, 256], P('col', 'row'), may hold values from -500 to 500
- target_features: bfloat16 [32768, 256], P(('row', 'col')), may hold values from -6 to 6
- weight: bfloat16 [256, 256], replicated, may hold values from -0.375 to 0.375
- score_source: float32 [4, 64], replicated, may hold values from -0.75 to 0.75
- score_target: float32 [4, 64], replicated, may hold values from -0.75 to 0.75
- out_bias: float32 [256], replicated, may hold values from -3 to 3
- block_list: int32 [32, 16, 48], P('row', 'col'), may hold values from 0 to 127, as said below
- block_count: int32 [32, 16], P('row', 'col'), may hold values from 8 to 48, as said below
- edge_bits: int32 [32, 16, 48, 16, 128], P('row', 'col'), may hold values from 0 to 255, as said below
Outputs:
- updated: bfloat16 [32768, 256], P(('row', 'col'))
Inputs may be any that keep to these rules, and one draw needn't show every extreme that they name: `block_list`: slot s of tile (r, c) names target block p // 16 and source block p % 16 of the tile; the first block_count[r, c] slots of a tile name distinct blocks and later slots are unused. `block_count`: some tile holds 48 blocks. `edge_bits`: bit b of entry [r, c, s, w, i] marks the edge from source 8 w + b to target i of the block in slot s. Some targets have no edge.
All inputs are finite; a program needn't handle non-finite values.
Results may differ from a plain program's by a relative error of at most 0.007.
The roundings to bfloat16 on the way count: a program that leaves them out, or rounds other values in their place, can miss the bound.
Values may be sent and summed in bfloat16 or wider, within the bound.
A program may use at most 64 MiB of HBM per device.

v0:
```python
import jax
import jax.numpy as jnp
from jax import lax
from jax.sharding import PartitionSpec as P

BLK = 128
SB = 16
very_low = -1e30
slope = 0.2


def unpack_all(packed):
    shifts = jnp.arange(8, dtype=jnp.int32)
    spread = jnp.right_shift(packed[:, :, None, :], shifts[None, None, :, None]) & 1
    return spread.reshape(packed.shape[0], packed.shape[1] * 8, packed.shape[2]) > 0


def all_scores(src_pick, dst_pick):
    raw = src_pick[:, :, :, None] + dst_pick[:, :, None, :]
    return jnp.where(raw > 0, raw, slope * raw)


def body(
    source_features,
    target_features,
    weight,
    score_source,
    score_target,
    out_bias,
    block_list,
    block_count,
    edge_bits,
):
    head_count = score_source.shape[0]
    head_size = score_source.shape[1]
    out_width = weight.shape[1]
    own_proj = jnp.dot(source_features[0], weight, preferred_element_type=jnp.float32).astype(
        jnp.bfloat16
    )
    projected = lax.all_gather(own_proj, "row", axis=0, tiled=True)
    src_logits = jnp.einsum(
        "nhk,hk->hn",
        projected.reshape(-1, head_count, head_size).astype(jnp.float32),
        score_source,
        precision=lax.Precision.HIGHEST,
    )
    dst_proj = jnp.dot(target_features, weight, preferred_element_type=jnp.float32)
    dst_local = jnp.einsum(
        "nhk,hk->hn",
        dst_proj.reshape(-1, head_count, head_size),
        score_target,
        precision=lax.Precision.HIGHEST,
    )
    dst_logits = lax.all_gather(dst_local, "col", axis=1, tiled=True)
    dst_rows = dst_logits.shape[1]
    dst_blocks_all = dst_rows // BLK
    src_blocks_all = src_logits.shape[1] // BLK
    slots = block_list[0, 0]
    live = block_count[0, 0]
    packed = edge_bits[0, 0]
    slot_count = slots.shape[0]
    dst_block = slots // SB
    src_block = slots % SB
    in_use = jnp.arange(slot_count, dtype=jnp.int32) < live
    edge_mask = unpack_all(packed) & in_use[:, None, None]
    src_pick = jnp.take(src_logits.reshape(head_count, src_blocks_all, BLK), src_block, axis=1)
    dst_pick = jnp.take(dst_logits.reshape(head_count, dst_blocks_all, BLK), dst_block, axis=1)
    owner = dst_block[:, None] == jnp.arange(dst_blocks_all, dtype=jnp.int32)[None, :]
    owner_float = owner.astype(jnp.float32)
    scores = all_scores(src_pick, dst_pick)
    block_max = jnp.max(jnp.where(edge_mask[None], scores, very_low), axis=2)
    spread_max = jnp.where(owner[None, :, :, None], block_max[:, :, None, :], very_low)
    row_max = jnp.max(spread_max, axis=1).reshape(head_count, dst_rows)
    row_max = lax.pmax(row_max, "col")
    prior_max = jnp.take(row_max.reshape(head_count, dst_blocks_all, BLK), dst_block, axis=1)
    scores = all_scores(src_pick, dst_pick)
    numer = jnp.exp(jnp.where(edge_mask[None], scores - prior_max[:, :, None, :], very_low))
    slot_denoms = jnp.sum(numer, axis=2)
    denoms = jnp.einsum(
        "sd,hsi->dih", owner_float, slot_denoms, precision=lax.Precision.HIGHEST
    ).reshape(dst_rows, head_count)
    weights = numer.astype(jnp.bfloat16)
    src_feats = jnp.take(
        projected.reshape(src_blocks_all, BLK, head_count, head_size), src_block, axis=0
    )
    product = jnp.einsum("hsji,sjhk->sihk", weights, src_feats, preferred_element_type=jnp.float32)
    accum = jnp.einsum(
        "sd,sihk->dihk", owner_float, product, precision=lax.Precision.HIGHEST
    ).reshape(dst_rows, out_width)
    accum, denoms = (
        lax.psum(accum.astype(jnp.bfloat16), "col").astype(jnp.float32),
        lax.psum(denoms.astype(jnp.bfloat16), "col").astype(jnp.float32),
    )
    own_count = dst_rows // lax.axis_size("col")
    first_row = lax.axis_index("col") * own_count
    accum = lax.dynamic_slice_in_dim(accum, first_row, own_count, 0)
    denoms = lax.dynamic_slice_in_dim(denoms, first_row, own_count, 0)
    own_count = accum.shape[0]
    blended = accum.reshape(own_count, head_count, head_size) / jnp.maximum(denoms, 1.0)[:, :, None]
    return jax.nn.elu(blended.reshape(own_count, out_width) + out_bias).astype(jnp.bfloat16)


def solution(mesh):
    placed = (
        P("col", "row", None),
        P(("row", "col"), None),
        P(),
        P(),
        P(),
        P(),
        P("row", "col", None),
        P("row", "col"),
        P("row", "col", None, None, None),
    )
    return jax.shard_map(
        body, mesh=mesh, in_specs=placed, out_specs=P(("row", "col"), None), check_vma=False
    )
```

profile of v0, /device:TPU:1, one launch (start us, length us, event | category | flops | bytes accessed | tf_op | source)
XLA Modules:
  0.0 296.6 jit_solution(9279656370350139183)
XLA Ops:
  6.5 0.0 copy-start
  6.5 0.0 all-gather.3.cloned.1.call-start
  6.5 0.9 copy-done
  7.4 1.5 convolution_convert_fusion
  9.0 0.0 all-gather.3.cloned.1.call-update
  9.0 0.0 all-reduce.2.cloned.1.call-start
  9.0 0.9 fusion.45
  9.9 0.1 reshape.177
  10.1 1.0 fusion.28
  11.1 24.6 %all-gather = f32[16,64,4]{1,2,0:T(4,128)S(1)} all-gather(f32[1,64,4]{1,2,0:T(4,128)S(1)} %bitcast.101), channel_id=1, replica_groups=mesh['row'=32,'col'=16] {'col'}, dimensions={0}, use_global_device_ids=true | all-gather | bytes 17408 | tf_op jit(solution)/shard_map/all_gather | solution.py:54
  35.6 0.1 reshape.217
  35.7 0.1 shift_right_arithmetic.30
  36.5 0.7 compare_and_fusion
  37.2 0.1 copy.42
  37.3 0.6 gather_fusion.2
  37.9 0.7 fusion.39
  38.6 1.9 fusion.17
  40.6 0.0 copy-start.2
  40.6 52.5 %all-gather.3.cloned.1.call-done = bf16[2048,256]{1,0:T(8,128)(2,1)} async-done(((bf16[64,256]{1,0:T(8,128)(2,1)}), bf16[2048,256]{1,0:T(8,128)(2,1)}) %all-gather.3.cloned.1.call-update) | async-done | bytes 1048592 | tf_op jit(solution)/shard_map/all_gather | solution.py:40
  93.1 1.6 copy.40
  94.7 1.2 fusion.44
  95.9 0.6 gather_fusion.1
  96.5 0.2 select_bitcast_fusion.1
  96.7 4.4 %select_reduce_fusion = f32[4,48,128]{2,0,1:T(4,128)S(1)} fusion(f32[4,48,128]{2,0,1:T(4,128)S(1)} %get-tuple-element.9, f32[4,48,128]{2,0,1:T(4,128)S(1)} %get-tuple-element.10, pred[48,128,128]{2,1,0:T(8,128)(4,1)S(1)} %fusion.17), kind=kLoop, calls=%fused_computation.6 | loop fusion | flops 18849792 | bytes 1081344 | tf_op jit(solution)/shard_map/reduce_max | solution.py:71
  101.1 0.1 select_reduce_fusion.1
  101.2 48.2 %pmax.7 = f32[4,8,128]{2,0,1:T(4,128)S(1)} all-reduce(f32[4,8,128]{2,0,1:T(4,128)S(1)} %copy.44), channel_id=1, replica_groups=mesh['row'=32,'col'=16] {'col'}, use_global_device_ids=true, to_apply=%region_2.4 | all-reduce | flops 4096 | bytes 32768 | tf_op jit(solution)/shard_map/pmax | solution.py:74
  149.4 0.6 gather_fusion.3
  150.1 0.0 copy-done.2
  150.1 0.8 select_bitcast_fusion
  150.8 0.0 copy-done.1
  150.8 0.8 reshape.228
  151.7 1.1 copy.39
  152.8 2.7 gather_fusion
  155.5 9.9 %fusion.18 = f32[48,128,4,64]{1,3,2,0:T(8,128)S(1)} fusion(f32[4,48,128]{2,0,1:T(4,128)S(1)} %copy-done.4, f32[4,48,128]{2,0,1:T(4,128)S(1)} %get-tuple-element.9, f32[4,48,128]{2,0,1:T(4,128)S(1)} %get-tuple-element.10, pred[48,128,128]{2,1,0:T(8,128)(4,1)S(1)} %copy-done.3, bf16[48,128,4,64]{1,3,2,0:T(8,128)(2,1)} %gather_fusion, ...), kind=kOutput, calls=%fused_computation.25 | convolution fusion | flops 426246144 | bytes 10518576 | tf_op jit(solution)/shard_map/hsji,sjhk->sihk/dot_general | solution.py:86
  165.4 0.0 copy-start.5
  165.4 5.7 %fusion.24 = bf16[8,128,4,64]{1,0,3,2:T(8,128)(2,1)S(1)} fusion(f32[48,128,4,64]{1,3,2,0:T(8,128)S(1)} %fusion.18, s32[48]{0:T(128)S(1)} %get-tuple-element.7), kind=kOutput, calls=%fused_computation.27 | convolution fusion | flops 151257472 | bytes 6815936 | tf_op jit(solution)/shard_map/sd,sihk->dihk/dot_general | solution.py:87
  171.1 0.1 copy.70
  171.2 1.0 copy.46
  172.2 0.0 all-reduce.2.cloned.1.call-update
  172.2 5.5 %fusion = f32[4,48,128]{2,0,1:T(4,128)S(1)} fusion(f32[4,48,128]{2,0,1:T(4,128)S(1)} %copy-done.4, f32[4,48,128]{2,0,1:T(4,128)S(1)} %get-tuple-element.9, f32[4,48,128]{2,0,1:T(4,128)S(1)} %get-tuple-element.10, pred[48,128,128]{2,1,0:T(8,128)(4,1)S(1)} %copy-done.3), kind=kLoop, calls=%fused_computation.7 | loop fusion | flops 21995520 | bytes 1179648 | tf_op jit(solution)/shard_map/reduce_sum | solution.py:78
  177.7 0.2 fusion.27
  177.9 27.0 %psum.15 = bf16[1024,4]{0,1:T(4,128)(2,1)S(1)} all-reduce(bf16[1024,4]{0,1:T(4,128)(2,1)S(1)} %bitcast.100), channel_id=1, replica_groups=mesh['row'=32,'col'=16] {'col'}, use_global_device_ids=true, to_apply=%region_5.7 | all-reduce | flops 4096 | bytes 16384 | tf_op jit(solution)/shard_map/psum | solution.py:92
  204.9 0.1 convert_maximum_fusion
  205.0 0.1 copy.48
  205.1 0.1 div.27
  205.2 0.1 div.28
  205.4 83.0 %all-reduce.2.cloned.1.call-done = bf16[1024,256]{1,0:T(8,128)(2,1)} async-done(((bf16[1024,256]{1,0:T(8,128)(2,1)}), bf16[1024,256]{1,0:T(8,128)(2,1)}) %all-reduce.2.cloned.1.call-update) | async-done | bytes 524304 | tf_op jit(solution)/shard_map/psum | solution.py:91
  288.3 1.4 fusion.32
  (17 shorter events, 0.1 us)
Async XLA Ops:
  6.5 0.9 copy-start
  6.5 86.5 %all-gather.3.cloned.1.call-start = ((), (), s32[]{:S(2)}) async-start(), calls=%async_computation | async-start | bytes 1081344 | tf_op jit(solution)/shard_map/all_gather | solution.py:40
  9.0 279.3 %all-reduce.2.cloned.1.call-start = ((), (), s32[]{:S(2)}) async-start(), calls=%async_computation.1 | async-start | bytes 1048576 | tf_op jit(solution)/shard_map/psum | solution.py:91
  40.6 109.5 %copy-start.2 = (pred[48,128,128]{2,1,0:T(8,128)(4,1)}, pred[48,128,128]{2,1,0:T(8,128)(4,1)S(1)}, u32[]{:S(2)}) copy-start(pred[48,128,128]{2,1,0:T(8,128)(4,1)S(1)} %fusion.17) | copy-start | bytes 2359300
  93.1 57.7 %copy-start.1 = (bf16[2048,256]{1,0:T(8,128)(2,1)S(1)}, bf16[2048,256]{1,0:T(8,128)(2,1)}, u32[]{:S(2)}) copy-start(bf16[2048,256]{1,0:T(8,128)(2,1)} %all-gather.3.cloned.1.call-done) | copy-start | bytes 3145732
  152.8 2.7 copy-start.3
  152.8 2.7 copy-start.4
  165.4 122.9 %copy-start.5 = (f32[256]{0:T(256)S(1)}, f32[256]{0:T(256)}, u32[]{:S(2)}) copy-start(f32[256]{0:T(256)} %param.16) | copy-start | bytes 3076
Sparse Core Ops, SparseCore 0:
  10.5 82.5 all-gather.2
  172.3 115.9 all-reduce.1
where the time goes:
time: 297 us
  waiting for transfers between devices  136 us (46%)
  blocking collectives  99.8 us (34%)
  matrix products  20.3 us (7%)
  other arithmetic  15.7 us (5%)
  between operations  14.3 us (5%)
  local copies, waits for them, and re-layouts  10.9 us (4%)
    psum x1, waiting for transfers between devices, body(): lax.psum(accum.astype(jnp.bfloat16), 'col').astype(jnp.float32)  83 us
    all_gather x1, waiting for transfers between devices, body(): projected = lax.all_gather(own_proj, 'row', axis=0, tiled=True)  52.5 us
    pmax x1, blocking collectives, body(): row_max = lax.pmax(row_max, 'col')  48.2 us
    psum x1, blocking collectives, body(): lax.psum(denoms.astype(jnp.bfloat16), 'col').astype(jnp.float32)  27 us
    all_gather x1, blocking collectives, body(): dst_logits = lax.all_gather(dst_local, 'col', axis=1, tiled=True)  24.6 us
    dot_general x1, matrix products, body(): jnp.einsum('hsji,sjhk->sihk', weights, src_feats, preferred_element_type=...  9.89 us
  transfers between devices with their start and end apart: 2, of which 2 were waited for; matrix products, arithmetic and copies ran while one was open for 4% of the time, Pallas kernels for 0%

commit v1 on v0

--- a/solution.py
+++ b/solution.py
@@ -7,6 +7,13 @@
 SB = 16
 very_low = -1e30
 slope = 0.2
+
+
+def trails_choose(page, ax_name):
+    front = lax.all_to_all(
+        jnp.stack([page] * lax.axis_size(ax_name)), axis_name=ax_name, split_axis=0, concat_axis=0
+    )
+    return jnp.concatenate(front, 0)
 
 
 def unpack_all(packed):
@@ -37,7 +44,7 @@
     own_proj = jnp.dot(source_features[0], weight, preferred_element_type=jnp.float32).astype(
         jnp.bfloat16
     )
-    projected = lax.all_gather(own_proj, "row", axis=0, tiled=True)
+    projected = trails_choose(own_proj, ax_name="row")
     src_logits = jnp.einsum(
         "nhk,hk->hn",
         projected.reshape(-1, head_count, head_size).astype(jnp.float32),

time: 297 us -> 253 us (0.85)
  waiting for transfers between devices: 136 us -> 80.1 us
  starting transfers between devices: 0.04 us -> 10.5 us
    all_gather x1 -> x0, waiting for transfers between devices: 52.5 us -> none  [body(): projected = lax.all_gather(own_proj, 'row', axis=0, tiled=True)]
    all_to_all x0 -> x1, starting transfers between devices: none -> 10.5 us  [trails_choose(): lax.all_to_all(jnp.stack([page] * lax.axis_size(ax_name)), axis_name=ax_n...]
    another operation x0 -> x4, local copies, waits for them, and re-layouts: none -> 4.92 us  [the longest x2 1.91 us: body(): projected.reshape(src_blocks_all, BLK, head_count, head_size)]
  transfers between devices with their start and end apart: 2 -> 2, of which waited for: 2 -> 1; matrix products, arithmetic and copies ran while one was open for 4% -> 5% of each run, Pallas kernels for 0% -> 0%
where the time goes in v1:
time: 253 us; the launch traced here: 252 us
  blocking collectives  97.3 us (38%)
  waiting for transfers between devices  80.1 us (32%)
  matrix products  21.8 us (9%)
  other arithmetic  15.7 us (6%)
  between operations  14.3 us (6%)
  local copies, waits for them, and re-layouts  12.4 us (5%)
  starting transfers between devices  10.5 us (4%)
    psum x1, waiting for transfers between devices, body(): lax.psum(accum.astype(jnp.bfloat16), 'col').astype(jnp.float32)  80 us
    pmax x1, blocking collectives, body(): row_max = lax.pmax(row_max, 'col')  46.3 us
    psum x1, blocking collectives, body(): lax.psum(denoms.astype(jnp.bfloat16), 'col').astype(jnp.float32)  26.9 us
    all_gather x1, blocking collectives, body(): dst_logits = lax.all_gather(dst_local, 'col', axis=1, tiled=True)  24 us
    all_to_all x1, starting transfers between devices, trails_choose(): lax.all_to_all(jnp.stack([page] * lax.axis_size(ax_name)), axis_name=ax_n...  10.5 us
    dot_general x1, matrix products, body(): jnp.einsum('hsji,sjhk->sihk', weights, src_feats, preferred_element_type=...  9.89 us
    dot_general x1, matrix products, body(): jnp.einsum('sd,sihk->dihk', owner_float, product, precision=lax.Precision...  5.67 us
    reduce_sum x1, other arithmetic, body(): slot_denoms = jnp.sum(numer, axis=2)  5.5 us
  transfers between devices with their start and end apart: 2, of which 1 were waited for; matrix products, arithmetic and copies ran while one was open for 5% of the time, Pallas kernels for 0%

profile of v1, /device:TPU:1, one launch (start us, length us, event | category | flops | bytes accessed | tf_op | source)
XLA Modules:
  0.0 252.1 jit_solution(1095672618639681363)
XLA Ops:
  6.5 0.0 copy-start
  6.5 0.9 copy-done
  7.4 0.9 convolution_convert_fusion
  8.3 1.1 stack.2
  9.5 10.5 %all-to-all-start = ((bf16[32,64,256]{2,1,0:T(8,128)(2,1)}), bf16[32,64,256]{2,1,0:T(8,128)(2,1)S(1)}, u32[]{:S(2)}, u32[]{:S(2)}) async-start(bf16[32,64,256]{2,1,0:T(8,128)(2,1)} %stack.2), calls=%async_computation | async-start | bytes 2097152 | tf_op jit(solution)/shard_map/all_to_all | solution.py:13
  20.0 0.0 all-reduce.2.cloned.1.call-start
  20.0 0.9 fusion.46
  20.9 0.1 reshape.171
  21.1 1.0 fusion.30
  22.0 24.0 %all-gather = f32[16,64,4]{1,2,0:T(4,128)S(1)} all-gather(f32[1,64,4]{1,2,0:T(4,128)S(1)} %bitcast.98), channel_id=1, replica_groups=mesh['row'=32,'col'=16] {'col'}, dimensions={0}, use_global_device_ids=true | all-gather | bytes 17408 | tf_op jit(solution)/shard_map/all_gather | solution.py:61
  46.1 0.1 reshape.211
  46.2 0.1 shift_right_arithmetic.30
  46.9 0.7 compare_and_fusion
  47.6 0.1 copy.40
  47.7 0.6 gather_fusion.2
  48.4 0.7 fusion.41
  49.0 1.9 fusion.17
  51.0 0.0 copy-start.1
  51.0 0.0 all-to-all-done
  51.0 1.9 reshape.223
  52.9 0.0 copy-done.5
  52.9 3.3 %fusion.23 = f32[4,1,2048]{2,1,0:T(1,128)S(1)} fusion(f32[4,64,1]{1,2,0:T(1,128)S(1)} %bitcast.100, bf16[2048,4,64]{2,1,0:T(4,128)(2,1)} %reshape.223), kind=kOutput, calls=%fused_computation.26 | convolution fusion | flops 6291456 | bytes 1082368 | tf_op jit(solution)/shard_map/nhk,hk->hn/dot_general | solution.py:48
  56.2 0.6 gather_fusion.1
  56.8 0.2 select_bitcast_fusion.1
  57.0 4.4 %select_reduce_fusion = f32[4,48,128]{2,0,1:T(4,128)S(1)} fusion(f32[4,48,128]{2,0,1:T(4,128)S(1)} %get-tuple-element.9, f32[4,48,128]{2,0,1:T(4,128)S(1)} %get-tuple-element.10, pred[48,128,128]{2,1,0:T(8,128)(4,1)S(1)} %fusion.17), kind=kLoop, calls=%fused_computation.6 | loop fusion | flops 18849792 | bytes 1081344 | tf_op jit(solution)/shard_map/reduce_max | solution.py:78
  61.4 0.1 select_reduce_fusion.1
  61.6 46.3 %pmax.7 = f32[4,8,128]{2,0,1:T(4,128)S(1)} all-reduce(f32[4,8,128]{2,0,1:T(4,128)S(1)} %copy.42), channel_id=1, replica_groups=mesh['row'=32,'col'=16] {'col'}, use_global_device_ids=true, to_apply=%region_2.4 | all-reduce | flops 4096 | bytes 32768 | tf_op jit(solution)/shard_map/pmax | solution.py:81
  107.9 0.6 gather_fusion.3
  108.6 0.8 select_bitcast_fusion
  109.3 0.8 reshape.222
  110.1 1.1 copy.37
  111.3 2.7 %gather_fusion = bf16[48,128,4,64]{1,3,2,0:T(8,128)(2,1)} fusion(bf16[16,128,4,64]{1,3,2,0:T(8,128)(2,1)S(1)} %copy.37, s32[1024]{0:T(1024)S(1)} %pad_clamp_fusion.1), kind=kCustom, calls=%fused_computation.2 | custom fusion | bytes 6291648 | tf_op jit(solution)/shard_map/jit(_take)/gather | solution.py:90
  114.0 0.0 copy-done.2
  114.0 9.9 %fusion.18 = f32[48,128,4,64]{1,3,2,0:T(8,128)S(1)} fusion(f32[4,48,128]{2,0,1:T(4,128)S(1)} %copy-done.3, f32[4,48,128]{2,0,1:T(4,128)S(1)} %get-tuple-element.9, f32[4,48,128]{2,0,1:T(4,128)S(1)} %get-tuple-element.10, pred[48,128,128]{2,1,0:T(8,128)(4,1)S(1)} %copy-done.2, bf16[48,128,4,64]{1,3,2,0:T(8,128)(2,1)} %gather_fusion, ...), kind=kOutput, calls=%fused_computation.25 | convolution fusion | flops 426246144 | bytes 10518576 | tf_op jit(solution)/shard_map/hsji,sjhk->sihk/dot_general | solution.py:93
  123.9 0.0 copy-start.4
  123.9 5.7 %fusion.26 = bf16[8,128,4,64]{1,0,3,2:T(8,128)(2,1)S(1)} fusion(f32[48,128,4,64]{1,3,2,0:T(8,128)S(1)} %fusion.18, s32[48]{0:T(128)S(1)} %get-tuple-element.7), kind=kOutput, calls=%fused_computation.29 | convolution fusion | flops 151257472 | bytes 6815936 | tf_op jit(solution)/shard_map/sd,sihk->dihk/dot_general | solution.py:94
  129.6 0.1 copy.71
  129.7 1.0 copy.44
  130.7 0.0 all-reduce.2.cloned.1.call-update
  130.7 5.5 %fusion = f32[4,48,128]{2,0,1:T(4,128)S(1)} fusion(f32[4,48,128]{2,0,1:T(4,128)S(1)} %copy-done.3, f32[4,48,128]{2,0,1:T(4,128)S(1)} %get-tuple-element.9, f32[4,48,128]{2,0,1:T(4,128)S(1)} %get-tuple-element.10, pred[48,128,128]{2,1,0:T(8,128)(4,1)S(1)} %copy-done.2), kind=kLoop, calls=%fused_computation.7 | loop fusion | flops 21995520 | bytes 1179648 | tf_op jit(solution)/shard_map/reduce_sum | solution.py:85
  136.2 0.2 fusion.29
  136.4 26.9 %psum.15 = bf16[1024,4]{0,1:T(4,128)(2,1)S(1)} all-reduce(bf16[1024,4]{0,1:T(4,128)(2,1)S(1)} %bitcast.97), channel_id=1, replica_groups=mesh['row'=32,'col'=16] {'col'}, use_global_device_ids=true, to_apply=%region_5.7 | all-reduce | flops 4096 | bytes 16384 | tf_op jit(solution)/shard_map/psum | solution.py:99
  163.3 0.1 convert_maximum_fusion
  163.4 0.1 copy.46
  163.5 0.1 div.27
  163.6 0.1 div.28
  163.8 80.0 %all-reduce.2.cloned.1.call-done = bf16[1024,256]{1,0:T(8,128)(2,1)} async-done(((bf16[1024,256]{1,0:T(8,128)(2,1)}), bf16[1024,256]{1,0:T(8,128)(2,1)}) %all-reduce.2.cloned.1.call-update) | async-done | bytes 524304 | tf_op jit(solution)/shard_map/psum | solution.py:98
  243.8 1.4 fusion.34
  (17 shorter events, 0.1 us)
Async XLA Ops:
  6.5 0.9 copy-start
  6.5 46.3 %copy-start.5 = (f32[4,64]{1,0:T(4,128)S(1)}, f32[4,64]{1,0:T(4,128)}, u32[]{:S(2)}) copy-start(f32[4,64]{1,0:T(4,128)} %param.14) | copy-start | bytes 3076
  9.5 41.5 %all-to-all-start = ((bf16[32,64,256]{2,1,0:T(8,128)(2,1)}), bf16[32,64,256]{2,1,0:T(8,128)(2,1)S(1)}, u32[]{:S(2)}, u32[]{:S(2)}) async-start(bf16[32,64,256]{2,1,0:T(8,128)(2,1)} %stack.2), calls=%async_computation | async-start | bytes 2097152 | tf_op jit(solution)/shard_map/all_to_all | solution.py:13
  20.0 223.8 %all-reduce.2.cloned.1.call-start = ((), (), s32[]{:S(2)}) async-start(), calls=%async_computation.1 | async-start | bytes 1048576 | tf_op jit(solution)/shard_map/psum | solution.py:98
  51.0 57.6 %copy-start.1 = (pred[48,128,128]{2,1,0:T(8,128)(4,1)}, pred[48,128,128]{2,1,0:T(8,128)(4,1)S(1)}, u32[]{:S(2)}) copy-start(pred[48,128,128]{2,1,0:T(8,128)(4,1)S(1)} %fusion.17) | copy-start | bytes 2359300
  111.2 2.7 %copy-start.2 = (pred[48,128,128]{2,1,0:T(8,128)(4,1)S(1)}, pred[48,128,128]{2,1,0:T(8,128)(4,1)}, u32[]{:S(2)}) copy-start(pred[48,128,128]{2,1,0:T(8,128)(4,1)} %copy-done.1) | copy-start | bytes 2359300
  111.2 2.7 %copy-start.3 = (f32[4,48,128]{2,0,1:T(4,128)S(1)}, f32[4,48,128]{2,0,1:T(4,128)}, u32[]{:S(2)}) copy-start(f32[4,48,128]{2,0,1:T(4,128)} %select_bitcast_fusion) | copy-start | bytes 294916
  123.9 119.9 %copy-start.4 = (f32[256]{0:T(256)S(1)}, f32[256]{0:T(256)}, u32[]{:S(2)}) copy-start(f32[256]{0:T(256)} %param.16) | copy-start | bytes 3076
Sparse Core Ops, SparseCore 0:
  130.8 112.9 all-reduce.1
